TPU v7x, 512 devices: a whole 4x8x8 slice. The times are simulated.
512 devices in a mesh: segment: 4 (over z_hi), seq: 32 (over y, x), dp: 4 (over z_lo, core).
Axes of the slice: x: 4, y: 8, z: 8 (z_hi: 4, z_lo: 2; z = z_hi * 2 + z_lo), core: 2. Of those that a mesh axis runs over, the one named last changes fastest.
Arguments:
- decoder_queries: bfloat16 [4, 4, 2048, 4096], P('segment', 'dp', None, 'seq'), may hold values from -95 to 95
- decoder_keys: bfloat16 [4, 4, 2048, 4096], P('segment', 'dp', None, 'seq'), may hold values from -2.1 to 2.1
- decoder_values: bfloat16 [4, 4, 2048, 4096], P('segment', 'dp', None, 'seq'), may hold values from -6 to 6
- cross_queries: bfloat16 [4, 4, 2048, 4096], P('segment', 'dp', None, 'seq'), may hold values from -95 to 95
- memory_keys: bfloat16 [4, 4, 2048, 512], P('segment', 'dp', None, 'seq'), may hold values from -2.1 to 2.1
- memory_values: bfloat16 [4, 4, 2048, 512], P('segment', 'dp', None, 'seq'), may hold values from -6 to 6
- target_lengths: int32 [4, 4, 2], P('segment', 'dp'), may hold values from 512 to 2048, as said below
- source_lengths: int32 [4, 4, 2], P('segment', 'dp'), may hold values from 64 to 256, as said below
Outputs:
- mixed: bfloat16 [4, 4, 2048, 4096], P('segment', 'dp', None, 'seq')
Inputs may be any that keep to these rules, and one draw needn't show every extreme that they name: `target_lengths`: some sequence has exactly 2048 live tokens and some other exactly 512. `source_lengths`: some sequence has exactly 256 live memory tokens and some other exactly 64.
All inputs are finite; a program needn't handle non-finite values.
Results may differ from a plain program's by a relative error of at most 0.0057.
Values may be sent and summed in bfloat16 or wider, within the bound.
A program may use at most 64 MiB of HBM per device.

v0:
```python
import functools

import jax
import jax.numpy as jnp
from jax import lax
from jax.experimental import pallas as pl
from jax.experimental.pallas import tpu as pltpu
from jax.sharding import PartitionSpec as P

HS = 64
SEQS = 2
BLOCK = 256
MASKED = -1e30
MESH = pl.DeviceIdType.MESH


def kernel(
    n_seg, n_seq, n_dp,
    target_ref, source_ref, dq_ref, dk_ref, dv_ref, cq_ref, mk_ref, mv_ref,
    out_ref,
    q_buf, k_buf, v_buf, c_buf, mk_buf, mv_buf, kt_buf, mvt_buf, o_buf, len_own, len_all,
    in_sems, mem_sem, len_sem, out_sem, send_sem, mem_send, len_send, out_send,
):
    group = n_seq // SEQS
    tokens = dq_ref.shape[1]
    seq_len = group * tokens
    mem_tokens = mk_ref.shape[0]
    heads = q_buf.shape[0]
    owned = heads * HS
    replicas = n_seg * n_dp

    seg, place, dp = lax.axis_index("segment"), lax.axis_index("seq"), lax.axis_index("dp")
    which = place // group
    rank = place % group
    first = which * group
    own = seg * n_dp + dp
    target = target_ref[0, 0, which]
    source = source_ref[0, 0, which]

    def partner(step):
        return (rank + step) % group

    def other(step):
        index = (own + step) % replicas
        return {"segment": index // n_dp, "dp": index % n_dp}

    later_seg = (seg + 1) % n_seg
    early_seg = (seg + n_seg - 1) % n_seg

    row = lax.broadcasted_iota(jnp.int32, (HS, seq_len), 0)
    column = lax.broadcasted_iota(jnp.int32, (HS, seq_len), 1)
    one_row = jnp.where(row == 0, 1.0, 0.0).astype(jnp.bfloat16)
    mask_row = jnp.where((row == 0) & (column >= target), MASKED, 0.0).astype(jnp.bfloat16)
    for h in range(heads):
        q_buf[h, HS:, :] = one_row
        k_buf[h, HS:, :] = mask_row
        v_buf[h, HS:, :] = one_row[:16]
        c_buf[h, (1 - h) * HS : (2 - h) * HS, :] = one_row
    lens = jnp.full(len_own.shape, target_ref[0, 0, 0] + target_ref[0, 0, 1], jnp.int32)
    len_own[...] = lens
    len_all[own] = lens

    barrier = pltpu.get_barrier_semaphore()

    @pl.loop(1, group)
    def _(step):
        pl.semaphore_signal(barrier, 1, device_id={"seq": first + partner(step)}, device_id_type=MESH)

    @pl.loop(0, group)
    def _(step):
        pl.semaphore_signal(
            barrier, 1, device_id={"segment": early_seg, "seq": first + step}, device_id_type=MESH
        )

    @pl.loop(1, replicas)
    def _(step):
        pl.semaphore_signal(barrier, 1, device_id=other(step), device_id_type=MESH)

    pl.semaphore_wait(barrier, 2 * group - 1 + replicas - 1)

    @pl.loop(1, replicas)
    def _(step):
        pltpu.make_async_remote_copy(
            src_ref=len_own, dst_ref=len_all.at[own], send_sem=len_send, recv_sem=len_sem,
            device_id=other(step), device_id_type=MESH,
        ).start()

    mem_rows = pl.ds(pl.multiple_of(rank * mem_tokens, mem_tokens), mem_tokens)

    @pl.loop(0, group)
    def _(step):
        to = partner(step)
        lanes = pl.ds(pl.multiple_of(to * owned, owned), owned)
        for pair, (src, dst) in enumerate(((mk_ref, mk_buf), (mv_ref, mv_buf))):
            pltpu.make_async_remote_copy(
                src_ref=src.at[:, lanes], dst_ref=dst.at[mem_rows],
                send_sem=mem_send.at[pair], recv_sem=mem_sem.at[pair],
                device_id={"segment": later_seg, "seq": first + to}, device_id_type=MESH,
            ).start()

    own_lanes = pl.ds(pl.multiple_of(rank * tokens, tokens), tokens)
    kinds = ((dk_ref, k_buf), (dv_ref, v_buf), (dq_ref, q_buf), (cq_ref, c_buf))

    def landing(kind, h):
        shift = h * HS if kind == 3 else 0
        return kinds[kind][1].at[h, pl.ds(shift, HS)]

    for h in range(heads):
        for kind in range(4):
            src = kinds[kind][0]
            dst = landing(kind, h).at[:, own_lanes]
            sem = in_sems.at[h, kind]
            pltpu.make_async_copy(
                src.at[pl.ds(pl.multiple_of(rank * owned, owned) + h * HS, HS)], dst, sem
            ).start()

            @pl.loop(1, group)
            def _(step):
                to = partner(step)
                pltpu.make_async_remote_copy(
                    src_ref=src.at[pl.ds(pl.multiple_of(to * owned, owned) + h * HS, HS)],
                    dst_ref=dst, send_sem=send_sem.at[kind], recv_sem=sem,
                    device_id={"seq": first + to}, device_id_type=MESH,
                ).start()

    pltpu.make_async_copy(len_all.at[pl.ds(1, replicas - 1)], len_all.at[pl.ds(1, replicas - 1)], len_sem).wait()
    live = jnp.sum(len_all[...], axis=0)[0:1]
    scale = jnp.float32(n_seg * n_dp * SEQS * seq_len) / live.astype(jnp.float32)
    scale = jnp.concatenate([scale] * (BLOCK // 128), axis=1)

    pltpu.make_async_copy(mk_buf, mk_buf, mem_sem.at[0]).wait()
    pltpu.make_async_copy(mv_buf, mv_buf, mem_sem.at[1]).wait()
    mem_len = mk_buf.shape[0]
    ones = jnp.where(lax.broadcasted_iota(jnp.int32, (16, mem_len), 0) == 0, 1.0, 0.0).astype(jnp.bfloat16)
    values_t = mv_buf[...].T
    for h in range(heads):
        mvt_buf[h] = jnp.concatenate([values_t[h * HS : (h + 1) * HS], ones], axis=0)
    lane = lax.broadcasted_iota(jnp.int32, (mem_len, owned), 1)
    token = lax.broadcasted_iota(jnp.int32, (mem_len, owned), 0)

    def attend(keys, queries, values, causal):
        scores = jnp.dot(keys, queries, preferred_element_type=jnp.float32)
        if causal:
            rows = scores.shape[0] - BLOCK
            i = lax.broadcasted_iota(jnp.int32, (BLOCK, BLOCK), 1)
            j = lax.broadcasted_iota(jnp.int32, (BLOCK, BLOCK), 0)
            last = jnp.where(j <= i, scores[rows:], MASKED)
            scores = jnp.concatenate([scores[:rows], last], axis=0) if rows else last
        highest = jnp.max(scores, axis=0, keepdims=True)
        weights = jnp.exp(scores - highest).astype(jnp.bfloat16)
        both = jnp.dot(values, weights, preferred_element_type=jnp.float32)
        context = both[:HS] / both[HS : HS + 1]
        return context

    for h in range(heads):
        for kind in range(4):
            sem = in_sems.at[h, kind]
            pltpu.make_async_copy(landing(kind, h), landing(kind, h), sem).wait()
        for j in range(0, seq_len, 128):
            kt_buf[j : j + 128, :] = k_buf[h, :, j : j + 128].T
        inside = (lane >= h * HS) & (lane < (h + 1) * HS)
        mask = jnp.where((lane == (1 - h) * HS) & (token >= source), MASKED, 0.0).astype(jnp.bfloat16)
        mem_keys = jnp.where(inside, mk_buf[...], mask)
        for b in range(seq_len // BLOCK):
            i0 = b * BLOCK
            self_part = attend(
                kt_buf[: i0 + BLOCK, :], q_buf[h, :, i0 : i0 + BLOCK], v_buf[h, :, : i0 + BLOCK], True
            )
            cross_part = attend(mem_keys, c_buf[h, :, i0 : i0 + BLOCK], mvt_buf[h], False)
            position = i0 + lax.broadcasted_iota(jnp.int32, (1, BLOCK), 1)
            weight = jnp.where(position < target, scale, 0.0)
            o_buf[h, :, i0 : i0 + BLOCK] = ((self_part + cross_part) * weight).astype(jnp.bfloat16)
            for to in range(i0 // tokens, (i0 + BLOCK) // tokens):
                src = o_buf.at[h, :, pl.ds(to * tokens, tokens)]
                dst = out_ref.at[pl.ds(pl.multiple_of(rank * owned, owned) + h * HS, HS)]

                @pl.when(rank != to)
                def _():
                    pltpu.make_async_remote_copy(
                        src_ref=src, dst_ref=dst, send_sem=out_send, recv_sem=out_sem,
                        device_id={"seq": first + to}, device_id_type=MESH,
                    ).start()

                @pl.when(rank == to)
                def _():
                    pltpu.make_async_copy(src, dst, out_sem).start()

    def drain(ref, sem):
        pltpu.make_async_copy(ref, ref, sem).wait()

    drain(len_all.at[pl.ds(1, replicas - 1)], len_send)
    drain(mk_buf, mem_send.at[0])
    drain(mv_buf, mem_send.at[1])
    for kind in range(4):
        drain(kinds[kind][1].at[:, pl.ds(0, HS), pl.ds(0, seq_len - tokens)], send_sem.at[kind])
    drain(o_buf.at[:, :, pl.ds(0, seq_len - tokens)], out_send)
    drain(out_ref, out_sem)


def local(n_seg, n_seq, n_dp, dq, dk, dv, cq, mk, mv, target, source):
    features, tokens = dq.shape[2:]
    group = n_seq // SEQS
    seq_len = group * tokens
    owned = features // group
    heads = owned // HS
    mem_tokens = mk.shape[3]
    flat = [a.reshape(features, tokens) for a in (dq, dk, dv, cq)]
    memory = [a.reshape(features, mem_tokens).T for a in (mk, mv)]
    bf16 = jnp.bfloat16
    dma = pltpu.SemaphoreType.DMA
    out = pl.pallas_call(
        functools.partial(kernel, n_seg, n_seq, n_dp),
        out_shape=jax.ShapeDtypeStruct((features, tokens), bf16),
        in_specs=[pl.BlockSpec(memory_space=pltpu.SMEM)] * 2 + [pl.BlockSpec(memory_space=pl.ANY)] * 6,
        out_specs=pl.BlockSpec(memory_space=pl.ANY),
        scratch_shapes=[
            pltpu.VMEM((heads, 2 * HS, seq_len), bf16),
            pltpu.VMEM((heads, 2 * HS, seq_len), bf16),
            pltpu.VMEM((heads, HS + 16, seq_len), bf16),
            pltpu.VMEM((heads, 2 * HS, seq_len), bf16),
            pltpu.VMEM((group * mem_tokens, owned), bf16),
            pltpu.VMEM((group * mem_tokens, owned), bf16),
            pltpu.VMEM((seq_len, 2 * HS), bf16),
            pltpu.VMEM((heads, HS + 16, group * mem_tokens), bf16),
            pltpu.VMEM((heads, HS, seq_len), bf16),
            pltpu.VMEM((8, 128), jnp.int32),
            pltpu.VMEM((n_seg * n_dp, 8, 128), jnp.int32),
            dma((heads, 4)), dma((2,)), dma, dma, dma((4,)), dma((2,)), dma, dma,
        ],
        compiler_params=pltpu.CompilerParams(
            collective_id=0, has_side_effects=True, vmem_limit_bytes=56 * 2**20
        ),
    )(target, source, *flat, *memory)
    return out.reshape(1, 1, features, tokens)


def solution(mesh):
    sizes = [mesh.shape[name] for name in ("segment", "seq", "dp")]
    wide = P("segment", "dp", None, "seq")
    in_specs = (wide,) * 6 + (P("segment", "dp", None),) * 2
    return jax.shard_map(
        functools.partial(local, *sizes), mesh=mesh, in_specs=in_specs, out_specs=wide, check_vma=False
    )
```

profile of v0, /device:TPU:56, one launch (start us, length us, event | category | flops | bytes accessed | tf_op | source)
XLA Modules:
  0.0 80.9 jit_solution(3808659830188443925)
XLA Ops:
  0.0 79.0 %shard_map.82 = bf16[2048,128]{1,0:T(8,128)(2,1)} custom-call(s32[1,1,2]{2,1,0:T(1,128)} %target_ref.1, s32[1,1,2]{2,1,0:T(1,128)} %source_ref.1, bf16[2048,128]{1,0:T(8,128)(2,1)} %bitcast.12, bf16[2048,128]{1,0:T(8,128)(2,1)} %bitcast.13, bf16[2048,128]{1,0:T(8,128)(2,1)} %bitcast.14, bf16[2048,128]{1,0:T(8,128)(2,1)} %bitcast.15, ...), custom_call_target="tpu_custom_call" | custom-call | tf_op jit(solution)/shard_map/pallas_call | solution.py:211
  79.0 1.9 %copy.10 = bf16[1,1,2048,128]{3,2,1,0:T(8,128)(2,1)} copy(bf16[1,1,2048,128]{3,2,1,0:T(8,128)(2,1)} %bitcast.11) | data formatting | bytes 1048576
where the time goes:
time: 81.6 us; the launch traced here: 80.9 us
  Pallas kernels  79 us (97%)
  local copies, waits for them, and re-layouts  1.87 us (2%)
    pallas_call x1, Pallas kernels, local(): pl.pallas_call(functools.partial(kernel, n_seg, n_seq, n_dp), out_shape=j...  79 us
    unnamed x1, local copies, waits for them, and re-layouts  1.87 us

commit v1 on v0

v1 whole, which is shorter than its diff:
```python
import functools

import jax
import jax.numpy as jnp
from jax import lax
from jax.experimental import pallas as pl
from jax.experimental.pallas import tpu as pltpu
from jax.sharding import PartitionSpec as P

HS = 64
SEQS = 2
BLOCK = 256
LANES = 128
MASKED = -1e30
MESH = pl.DeviceIdType.MESH
K, V, QU, Q, C = range(5)


def kernel(
    n_seg, n_seq, n_dp,
    target_ref, source_ref, dq_ref, dk_ref, dv_ref, cq_ref, mk_ref, mv_ref,
    out_ref,
    q_buf, k_buf, v_buf, c_buf, u_buf, rk_buf, rv_buf, mk_buf, mv_buf, kt_buf, mvt_buf,
    o_buf, part_buf, stat_buf, part_in, stat_in, acc_buf, len_own, len_dp, len_ring,
    in_sems, send_sems, relay_sems, relay_sends, mem_sems, mem_sends, part_sems, stat_sems,
    part_send, stat_send, dp_sem, dp_send, ring_sems, ring_sends, out_sem, out_send,
):
    group = n_seq // SEQS
    pair = group // 2
    tokens = dq_ref.shape[1]
    span = pair * tokens
    seq_len = group * tokens
    mem_tokens = mk_ref.shape[0]
    heads = q_buf.shape[0]
    owned = heads * HS
    blocks = span // BLOCK

    seg, place, dp = lax.axis_index("segment"), lax.axis_index("seq"), lax.axis_index("dp")
    which = place // group
    rank = place % group
    first = which * group
    upper = rank // pair
    part = rank % pair
    base = first + upper * pair
    target = target_ref[0, 0, which]
    source = source_ref[0, 0, which]
    later = {"segment": (seg + 1) % n_seg}
    early = {"segment": (seg + n_seg - 1) % n_seg}

    row = lax.broadcasted_iota(jnp.int32, (HS, span), 0)
    column = upper * span + lax.broadcasted_iota(jnp.int32, (HS, span), 1)
    one_row = jnp.where(row == 0, 1.0, 0.0).astype(jnp.bfloat16)
    mask_row = jnp.where((row == 0) & (column >= target), MASKED, 0.0).astype(jnp.bfloat16)
    for h in range(heads):
        q_buf[h, HS:, :] = one_row
        u_buf[h, HS:, :] = one_row
        k_buf[h, HS:, :] = mask_row
        v_buf[h, HS:, :] = one_row[:16]
        c_buf[h, (1 - h % 2) * HS : (2 - h % 2) * HS, :] = one_row
    lens = jnp.full(len_own.shape, target_ref[0, 0, 0] + target_ref[0, 0, 1], jnp.int32)
    len_own[...] = lens
    len_dp[dp] = lens

    barrier = pltpu.get_barrier_semaphore()

    @pl.loop(1, group)
    def _(step):
        pl.semaphore_signal(
            barrier, 1, device_id={"seq": first + (rank + step) % group}, device_id_type=MESH
        )

    for step in range(1, n_dp):
        pl.semaphore_signal(barrier, 1, device_id={"dp": (dp + step) % n_dp}, device_id_type=MESH)
    pl.semaphore_signal(barrier, 1, device_id=early, device_id_type=MESH)
    pl.semaphore_wait(barrier, group - 1 + n_dp - 1 + 1)

    def remote(src, dst, send, recv, device):
        pltpu.make_async_remote_copy(
            src_ref=src, dst_ref=dst, send_sem=send, recv_sem=recv, device_id=device, device_id_type=MESH
        ).start()

    def drain(ref, sem):
        pltpu.make_async_copy(ref, ref, sem).wait()

    def aligned(index, size):
        return pl.ds(pl.multiple_of(index, size), size)

    for step in range(1, n_dp):
        remote(len_own, len_dp.at[dp], dp_send, dp_sem, {"dp": (dp + step) % n_dp})
    for pos, (src, dst) in enumerate(((mk_ref, rk_buf), (mv_ref, rv_buf))):
        remote(src, dst, relay_sends.at[pos], relay_sems.at[pos], later)

    lanes_own = aligned(part * tokens, tokens)
    kinds = {K: (dk_ref, k_buf), V: (dv_ref, v_buf), QU: (dq_ref, u_buf), Q: (dq_ref, q_buf), C: (cq_ref, c_buf)}

    def send_head(h):
        for kind in (K, V, QU, Q, C):
            src, buf = kinds[kind]
            shift = (h % 2) * HS if kind == C else 0
            dst = buf.at[h, pl.ds(shift, HS), lanes_own]
            sem = in_sems.at[h, kind]

            def rows(to):
                return src.at[pl.ds(pl.multiple_of(to * owned, owned) + h * HS, HS)]

            if kind == QU:

                @pl.when(upper == 1)
                def _():
                    @pl.loop(0, pair)
                    def _(step):
                        to = (part + step) % pair
                        remote(rows(to), dst, send_sems.at[kind], sem, {"seq": first + to})

                continue

            pltpu.make_async_copy(rows(part), dst, sem).start()

            @pl.loop(1, pair)
            def _(step):
                to = (part + step) % pair
                remote(rows(to), dst, send_sems.at[kind], sem, {"seq": base + to})

    send_head(0)
    drain(len_dp.at[pl.ds(1, n_dp - 1)], dp_sem)
    len_ring[0] = jnp.sum(len_dp[...], axis=0)
    remote(len_ring.at[0], len_ring.at[1], ring_sends.at[0], ring_sems.at[0], later)
    send_head(1)
    drain(rk_buf, relay_sems.at[0])
    drain(rv_buf, relay_sems.at[1])
    mem_rows = aligned(rank * mem_tokens, mem_tokens)

    def spread(to, move):
        for pos, (src, dst) in enumerate(((rk_buf, mk_buf), (rv_buf, mv_buf))):
            for couple in range(heads // 2):
                start = pl.multiple_of((to % pair) * owned, owned) + couple * LANES
                move(src.at[:, pl.ds(start, LANES)], dst.at[couple, mem_rows], pos)

    spread(rank, lambda src, dst, pos: pltpu.make_async_copy(src, dst, mem_sems.at[pos]).start())

    @pl.loop(1, group)
    def _(step):
        to = (rank + step) % group
        spread(
            to,
            lambda src, dst, pos: remote(src, dst, mem_sends.at[pos], mem_sems.at[pos], {"seq": first + to}),
        )

    for hop in range(1, n_seg):
        drain(len_ring.at[hop], ring_sems.at[hop - 1])
        if hop < n_seg - 1:
            remote(len_ring.at[hop], len_ring.at[hop + 1], ring_sends.at[hop], ring_sems.at[hop], later)
        if hop == 1:
            for h in range(2, heads):
                send_head(h)

    live = jnp.sum(len_ring[...], axis=0)[0:1]
    scale = jnp.float32(n_seg * n_dp * SEQS * seq_len) / live.astype(jnp.float32)
    scale = jnp.concatenate([scale] * (BLOCK // LANES), axis=1)

    def attend(keys, queries, values, causal):
        scores = jnp.dot(keys, queries, preferred_element_type=jnp.float32)
        if causal:
            rows = scores.shape[0] - BLOCK
            i = lax.broadcasted_iota(jnp.int32, (BLOCK, BLOCK), 1)
            j = lax.broadcasted_iota(jnp.int32, (BLOCK, BLOCK), 0)
            last = jnp.where(j <= i, scores[rows:], MASKED)
            scores = jnp.concatenate([scores[:rows], last], axis=0) if rows else last
        highest = jnp.max(scores, axis=0, keepdims=True)
        weights = jnp.exp(scores - highest).astype(jnp.bfloat16)
        both = jnp.dot(values, weights, preferred_element_type=jnp.float32)
        return both[:HS], both[HS : HS + 1], highest

    def causal_block(h, b):
        upto = (b + 1) * BLOCK
        return attend(kt_buf[:upto], q_buf[h, :, b * BLOCK : upto], v_buf[h, :, :upto], True)

    mem_len = mk_buf.shape[1]
    lane = lax.broadcasted_iota(jnp.int32, (mem_len, LANES), 1)
    token = lax.broadcasted_iota(jnp.int32, (mem_len, LANES), 0)
    part_bytes = part_buf.at[0]

    def finish(h, b, self_part, mem_keys):
        i0 = b * BLOCK
        both, summed, _ = attend(mem_keys, c_buf[h, :, i0 : i0 + BLOCK], mvt_buf[h], False)
        position = upper * span + i0 + lax.broadcasted_iota(jnp.int32, (1, BLOCK), 1)
        weight = jnp.where(position < target, scale, 0.0)
        o_buf[h, :, i0 : i0 + BLOCK] = ((self_part + both / summed) * weight).astype(jnp.bfloat16)
        dst = out_ref.at[pl.ds(pl.multiple_of(part * owned + h * HS, HS), HS)]
        for to in range(i0 // tokens, (i0 + BLOCK) // tokens):
            src = o_buf.at[h, :, pl.ds(to * tokens, tokens)]

            @pl.when(part != to)
            def _():
                remote(src, dst, out_send, out_sem, {"seq": base + to})

            @pl.when(part == to)
            def _():
                pltpu.make_async_copy(src, dst, out_sem).start()

    def memory_keys(h):
        side = h % 2
        inside = (lane >= side * HS) & (lane < (side + 1) * HS)
        mask = jnp.where((lane == (1 - side) * HS) & (token >= source), MASKED, 0.0)
        return jnp.where(inside, mk_buf[h // 2], mask.astype(jnp.bfloat16))

    def merge_head(h):
        drain(part_bytes, part_sems.at[h])
        drain(stat_buf.at[0], stat_sems.at[h])
        mem_keys = memory_keys(h)
        for b in range(blocks):
            cols = slice(b * BLOCK, (b + 1) * BLOCK)
            per = BLOCK // LANES

            def stat(ref, at):
                return jnp.concatenate([ref[h, at + b * per + e : at + b * per + e + 1, :] for e in range(per)], axis=1)

            half = stat_buf.shape[1] // 2
            high_u, sum_u = stat(stat_buf, 0), stat(stat_buf, half)
            high_l, sum_l = stat(stat_in, 0), stat(stat_in, half)
            highest = jnp.maximum(high_u, high_l)
            keep_u, keep_l = jnp.exp(high_u - highest), sum_l * jnp.exp(high_l - highest)
            total = sum_u * keep_u + keep_l
            merged = acc_buf[h, :, cols] * (keep_u / total) + part_in[h, :, cols].astype(jnp.float32) * (keep_l / total)
            finish(h, b, merged, mem_keys)

    def put_stat(h, b, highest, summed):
        per = BLOCK // LANES
        half = stat_buf.shape[1] // 2
        for e in range(per):
            cols = slice(e * LANES, (e + 1) * LANES)
            stat_buf[h, b * per + e : b * per + e + 1, :] = highest[:, cols]
            stat_buf[h, half + b * per + e : half + b * per + e + 1, :] = summed[:, cols]

    def wait_input(h, kind):
        drain(part_bytes, in_sems.at[h, kind])

    drain(mk_buf, mem_sems.at[0])
    drain(mv_buf, mem_sems.at[1])
    ones = jnp.where(lax.broadcasted_iota(jnp.int32, (16, mem_len), 0) == 0, 1.0, 0.0).astype(jnp.bfloat16)
    for couple in range(heads // 2):
        values_t = mv_buf[couple].T
        for side in range(2):
            mvt_buf[2 * couple + side] = jnp.concatenate([values_t[side * HS : (side + 1) * HS], ones], axis=0)

    @pl.loop(0, heads)
    def _(h):
        wait_input(h, K)
        wait_input(h, V)
        for j in range(0, span, LANES):
            kt_buf[j : j + LANES, :] = k_buf[h, :, j : j + LANES].T

        @pl.when(upper == 0)
        def _():
            wait_input(h, QU)
            opposite = {"seq": place + pair}
            for b in range(blocks):
                cols = slice(b * BLOCK, (b + 1) * BLOCK)
                both, summed, highest = attend(kt_buf[...], u_buf[h, :, cols], v_buf[h], False)
                part_buf[h, :, cols] = (both / summed).astype(jnp.bfloat16)
                put_stat(h, b, highest, summed)
                span_cols = pl.ds(b * BLOCK, BLOCK)
                remote(part_buf.at[h, :, span_cols], part_in.at[h, :, span_cols], part_send, part_sems.at[h], opposite)
            remote(stat_buf.at[h], stat_in.at[h], stat_send, stat_sems.at[h], opposite)
            wait_input(h, Q)
            wait_input(h, C)
            mem_keys = memory_keys(h)
            for b in range(blocks):
                both, summed, _ = causal_block(h, b)
                finish(h, b, both / summed, mem_keys)

        @pl.when(upper == 1)
        def _():
            wait_input(h, Q)
            wait_input(h, C)
            for b in range(blocks):
                both, summed, highest = causal_block(h, b)
                acc_buf[h, :, b * BLOCK : (b + 1) * BLOCK] = both
                put_stat(h, b, highest, summed)

            @pl.when(h > 0)
            def _():
                merge_head(h - 1)

    @pl.when(upper == 1)
    def _():
        merge_head(heads - 1)
        drain(part_buf, send_sems.at[QU])

    @pl.when(upper == 0)
    def _():
        drain(part_buf, part_send)
        drain(stat_buf, stat_send)

    if n_dp > 1:
        drain(len_dp.at[pl.ds(1, n_dp - 1)], dp_send)
    for hop in range(n_seg - 1):
        drain(len_ring.at[hop], ring_sends.at[hop])
    drain(rk_buf, relay_sends.at[0])
    drain(rv_buf, relay_sends.at[1])
    for pos, buf in enumerate((mk_buf, mv_buf)):
        drain(buf.at[:, pl.ds(0, mem_len - mem_tokens)], mem_sends.at[pos])
    for kind in (K, V, Q, C):
        drain(part_buf.at[:, :, pl.ds(0, span - tokens)], send_sems.at[kind])
    drain(o_buf.at[:, :, pl.ds(0, span - tokens)], out_send)
    drain(out_ref, out_sem)


def local(n_seg, n_seq, n_dp, dq, dk, dv, cq, mk, mv, target, source):
    features, tokens = dq.shape[2:]
    group = n_seq // SEQS
    pair = group // 2
    span = pair * tokens
    owned = features // pair
    heads = owned // HS
    mem_tokens = mk.shape[3]
    mem_len = group * mem_tokens
    flat = [a.reshape(features, tokens) for a in (dq, dk, dv, cq)]
    memory = [a.reshape(features, mem_tokens).T for a in (mk, mv)]
    bf16, f32, i32 = jnp.bfloat16, jnp.float32, jnp.int32
    dma = pltpu.SemaphoreType.DMA
    wide = pltpu.VMEM((heads, 2 * HS, span), bf16)
    block = pltpu.VMEM((heads, HS, span), bf16)
    stats = pltpu.VMEM((heads, 2 * span // LANES, LANES), f32)
    relay = pltpu.VMEM((mem_tokens, features), bf16)
    memories = pltpu.VMEM((heads // 2, mem_len, LANES), bf16)
    out = pl.pallas_call(
        functools.partial(kernel, n_seg, n_seq, n_dp),
        out_shape=jax.ShapeDtypeStruct((features, tokens), bf16),
        in_specs=[pl.BlockSpec(memory_space=pltpu.SMEM)] * 2 + [pl.BlockSpec(memory_space=pl.ANY)] * 6,
        out_specs=pl.BlockSpec(memory_space=pl.ANY),
        scratch_shapes=[
            wide, wide, pltpu.VMEM((heads, HS + 16, span), bf16), wide, wide,
            relay, relay, memories, memories,
            pltpu.VMEM((span, 2 * HS), bf16),
            pltpu.VMEM((heads, HS + 16, mem_len), bf16),
            block, block, stats, block, stats,
            pltpu.VMEM((heads, HS, span), f32),
            pltpu.VMEM((8, LANES), i32),
            pltpu.VMEM((n_dp, 8, LANES), i32),
            pltpu.VMEM((n_seg, 8, LANES), i32),
            dma((heads, 5)), dma((5,)), dma((2,)), dma((2,)), dma((2,)), dma((2,)), dma((heads,)), dma((heads,)),
            dma, dma, dma, dma, dma((n_seg,)), dma((n_seg,)), dma, dma,
        ],
        compiler_params=pltpu.CompilerParams(
            collective_id=0, has_side_effects=True, vmem_limit_bytes=56 * 2**20
        ),
    )(target, source, *flat, *memory)
    return out.reshape(1, 1, features, tokens)


def solution(mesh):
    sizes = [mesh.shape[name] for name in ("segment", "seq", "dp")]
    wide = P("segment", "dp", None, "seq")
    in_specs = (wide,) * 6 + (P("segment", "dp", None),) * 2
    return jax.shard_map(
        functools.partial(local, *sizes), mesh=mesh, in_specs=in_specs, out_specs=wide, check_vma=False
    )
```

time: 81.6 us -> 72 us (0.88)
  the two profiles are of different devices: /device:TPU:56 before, /device:TPU:184 now
where the time goes in v1:
time: 72 us; the launch traced here: 71.8 us
  Pallas kernels  69.9 us (97%)
  local copies, waits for them, and re-layouts  1.87 us (3%)
    pallas_call x1, Pallas kernels, local(): pl.pallas_call(functools.partial(kernel, n_seg, n_seq, n_dp), out_shape=j...  69.9 us
    unnamed x1, local copies, waits for them, and re-layouts  1.87 us

profile of v1, /device:TPU:184, one launch (start us, length us, event | category | flops | bytes accessed | tf_op | source)
XLA Modules:
  0.0 71.8 jit_solution(4476561195697210166)
XLA Ops:
  0.0 69.9 %shard_map.82 = bf16[2048,128]{1,0:T(8,128)(2,1)} custom-call(s32[1,1,2]{2,1,0:T(1,128)} %target_ref.1, s32[1,1,2]{2,1,0:T(1,128)} %source_ref.1, bf16[2048,128]{1,0:T(8,128)(2,1)} %bitcast.12, bf16[2048,128]{1,0:T(8,128)(2,1)} %bitcast.13, bf16[2048,128]{1,0:T(8,128)(2,1)} %bitcast.14, bf16[2048,128]{1,0:T(8,128)(2,1)} %bitcast.15, ...), custom_call_target="tpu_custom_call" | custom-call | tf_op jit(solution)/shard_map/pallas_call | solution.py:327
  69.9 1.9 %copy.10 = bf16[1,1,2048,128]{3,2,1,0:T(8,128)(2,1)} copy(bf16[1,1,2048,128]{3,2,1,0:T(8,128)(2,1)} %bitcast.11) | data formatting | bytes 1048576

commit v2 on v1

--- a/solution.py
+++ b/solution.py
@@ -9,7 +9,7 @@
 
 HS = 64
 SEQS = 2
-BLOCK = 256
+BLOCK = 512
 LANES = 128
 MASKED = -1e30
 MESH = pl.DeviceIdType.MESH
@@ -21,7 +21,7 @@
     target_ref, source_ref, dq_ref, dk_ref, dv_ref, cq_ref, mk_ref, mv_ref,
     out_ref,
     q_buf, k_buf, v_buf, c_buf, u_buf, rk_buf, rv_buf, mk_buf, mv_buf, kt_buf, mvt_buf,
-    o_buf, part_buf, stat_buf, part_in, stat_in, acc_buf, len_own, len_dp, len_ring,
+    o_buf, part_buf, stat_buf, part_in, stat_in, acc_buf, cross_buf, len_own, len_dp, len_ring,
     in_sems, send_sems, relay_sems, relay_sends, mem_sems, mem_sends, part_sems, stat_sems,
     part_send, stat_send, dp_sem, dp_send, ring_sems, ring_sends, out_sem, out_send,
 ):
@@ -34,6 +34,7 @@
     heads = q_buf.shape[0]
     owned = heads * HS
     blocks = span // BLOCK
+    per = span // LANES
 
     seg, place, dp = lax.axis_index("segment"), lax.axis_index("seq"), lax.axis_index("dp")
     which = place // group
@@ -46,6 +47,18 @@
     source = source_ref[0, 0, which]
     later = {"segment": (seg + 1) % n_seg}
     early = {"segment": (seg + n_seg - 1) % n_seg}
+
+    barrier = pltpu.get_barrier_semaphore()
+
+    @pl.loop(1, group)
+    def _(step):
+        pl.semaphore_signal(
+            barrier, 1, device_id={"seq": first + (rank + step) % group}, device_id_type=MESH
+        )
+
+    for step in range(1, n_dp):
+        pl.semaphore_signal(barrier, 1, device_id={"dp": (dp + step) % n_dp}, device_id_type=MESH)
+    pl.semaphore_signal(barrier, 1, device_id=early, device_id_type=MESH)
 
     row = lax.broadcasted_iota(jnp.int32, (HS, span), 0)
     column = upper * span + lax.broadcasted_iota(jnp.int32, (HS, span), 1)
@@ -61,17 +74,6 @@
     len_own[...] = lens
     len_dp[dp] = lens
 
-    barrier = pltpu.get_barrier_semaphore()
-
-    @pl.loop(1, group)
-    def _(step):
-        pl.semaphore_signal(
-            barrier, 1, device_id={"seq": first + (rank + step) % group}, device_id_type=MESH
-        )
-
-    for step in range(1, n_dp):
-        pl.semaphore_signal(barrier, 1, device_id={"dp": (dp + step) % n_dp}, device_id_type=MESH)
-    pl.semaphore_signal(barrier, 1, device_id=early, device_id_type=MESH)
     pl.semaphore_wait(barrier, group - 1 + n_dp - 1 + 1)
 
     def remote(src, dst, send, recv, device):
@@ -82,8 +84,8 @@
     def drain(ref, sem):
         pltpu.make_async_copy(ref, ref, sem).wait()
 
-    def aligned(index, size):
-        return pl.ds(pl.multiple_of(index, size), size)
+    def aligned(start, size):
+        return pl.ds(pl.multiple_of(start, size), size)
 
     for step in range(1, n_dp):
         remote(len_own, len_dp.at[dp], dp_send, dp_sem, {"dp": (dp + step) % n_dp})
@@ -93,8 +95,8 @@
     lanes_own = aligned(part * tokens, tokens)
     kinds = {K: (dk_ref, k_buf), V: (dv_ref, v_buf), QU: (dq_ref, u_buf), Q: (dq_ref, q_buf), C: (cq_ref, c_buf)}
 
-    def send_head(h):
-        for kind in (K, V, QU, Q, C):
+    def send_head(h, which_kinds):
+        for kind in which_kinds:
             src, buf = kinds[kind]
             shift = (h % 2) * HS if kind == C else 0
             dst = buf.at[h, pl.ds(shift, HS), lanes_own]
@@ -121,11 +123,13 @@
                 to = (part + step) % pair
                 remote(rows(to), dst, send_sems.at[kind], sem, {"seq": base + to})
 
-    send_head(0)
+    first_kinds, last_kinds = (K, V, QU), (Q, C)
+    send_head(0, first_kinds)
     drain(len_dp.at[pl.ds(1, n_dp - 1)], dp_sem)
     len_ring[0] = jnp.sum(len_dp[...], axis=0)
     remote(len_ring.at[0], len_ring.at[1], ring_sends.at[0], ring_sems.at[0], later)
-    send_head(1)
+    send_head(1, first_kinds)
+    send_head(0, last_kinds)
     drain(rk_buf, relay_sems.at[0])
     drain(rv_buf, relay_sems.at[1])
     mem_rows = aligned(rank * mem_tokens, mem_tokens)
@@ -152,11 +156,14 @@
             remote(len_ring.at[hop], len_ring.at[hop + 1], ring_sends.at[hop], ring_sems.at[hop], later)
         if hop == 1:
             for h in range(2, heads):
-                send_head(h)
+                send_head(h, first_kinds)
+                send_head(h - 1, last_kinds)
+            send_head(heads - 1, last_kinds)
 
     live = jnp.sum(len_ring[...], axis=0)[0:1]
     scale = jnp.float32(n_seg * n_dp * SEQS * seq_len) / live.astype(jnp.float32)
-    scale = jnp.concatenate([scale] * (BLOCK // LANES), axis=1)
+    position = upper * span + lax.broadcasted_iota(jnp.int32, (1, span), 1)
+    weight = jnp.where(position < target, jnp.concatenate([scale] * per, axis=1), 0.0)
 
     def attend(keys, queries, values, causal):
         scores = jnp.dot(keys, queries, preferred_element_type=jnp.float32)
@@ -173,30 +180,30 @@
 
     def causal_block(h, b):
         upto = (b + 1) * BLOCK
-        return attend(kt_buf[:upto], q_buf[h, :, b * BLOCK : upto], v_buf[h, :, :upto], True)
+        return attend(kt_buf[h, :upto], q_buf[h, :, b * BLOCK : upto], v_buf[h, :, :upto], True)
 
     mem_len = mk_buf.shape[1]
     lane = lax.broadcasted_iota(jnp.int32, (mem_len, LANES), 1)
     token = lax.broadcasted_iota(jnp.int32, (mem_len, LANES), 0)
     part_bytes = part_buf.at[0]
 
-    def finish(h, b, self_part, mem_keys):
-        i0 = b * BLOCK
-        both, summed, _ = attend(mem_keys, c_buf[h, :, i0 : i0 + BLOCK], mvt_buf[h], False)
-        position = upper * span + i0 + lax.broadcasted_iota(jnp.int32, (1, BLOCK), 1)
-        weight = jnp.where(position < target, scale, 0.0)
-        o_buf[h, :, i0 : i0 + BLOCK] = ((self_part + both / summed) * weight).astype(jnp.bfloat16)
+    def finish(h, self_part, cross_part):
+        o_buf[h] = ((self_part + cross_part) * weight).astype(jnp.bfloat16)
         dst = out_ref.at[pl.ds(pl.multiple_of(part * owned + h * HS, HS), HS)]
-        for to in range(i0 // tokens, (i0 + BLOCK) // tokens):
-            src = o_buf.at[h, :, pl.ds(to * tokens, tokens)]
-
-            @pl.when(part != to)
-            def _():
-                remote(src, dst, out_send, out_sem, {"seq": base + to})
-
-            @pl.when(part == to)
-            def _():
-                pltpu.make_async_copy(src, dst, out_sem).start()
+        pltpu.make_async_copy(o_buf.at[h, :, lanes_own], dst, out_sem).start()
+
+        @pl.loop(1, pair)
+        def _(step):
+            to = (part + step) % pair
+            remote(o_buf.at[h, :, aligned(to * tokens, tokens)], dst, out_send, out_sem, {"seq": base + to})
+
+    def cross(h):
+        both, summed, _ = attend(memory_keys(h), c_buf[h], mvt_buf[h], False)
+        return both / summed
+
+    def causal(h):
+        pieces = [causal_block(h, b) for b in range(blocks)]
+        return [jnp.concatenate([piece[k] for piece in pieces], axis=1) for k in range(3)]
 
     def memory_keys(h):
         side = h % 2
@@ -204,33 +211,26 @@
         mask = jnp.where((lane == (1 - side) * HS) & (token >= source), MASKED, 0.0)
         return jnp.where(inside, mk_buf[h // 2], mask.astype(jnp.bfloat16))
 
+    def put_stat(h, highest, summed):
+        for e in range(per):
+            cols = slice(e * LANES, (e + 1) * LANES)
+            stat_buf[h, e : e + 1, :] = highest[:, cols]
+            stat_buf[h, per + e : per + e + 1, :] = summed[:, cols]
+
+    def get_stat(ref, h):
+        wide = [jnp.concatenate([ref[h, at + e : at + e + 1, :] for e in range(per)], axis=1) for at in (0, per)]
+        return wide
+
     def merge_head(h):
         drain(part_bytes, part_sems.at[h])
         drain(stat_buf.at[0], stat_sems.at[h])
-        mem_keys = memory_keys(h)
-        for b in range(blocks):
-            cols = slice(b * BLOCK, (b + 1) * BLOCK)
-            per = BLOCK // LANES
-
-            def stat(ref, at):
-                return jnp.concatenate([ref[h, at + b * per + e : at + b * per + e + 1, :] for e in range(per)], axis=1)
-
-            half = stat_buf.shape[1] // 2
-            high_u, sum_u = stat(stat_buf, 0), stat(stat_buf, half)
-            high_l, sum_l = stat(stat_in, 0), stat(stat_in, half)
-            highest = jnp.maximum(high_u, high_l)
-            keep_u, keep_l = jnp.exp(high_u - highest), sum_l * jnp.exp(high_l - highest)
-            total = sum_u * keep_u + keep_l
-            merged = acc_buf[h, :, cols] * (keep_u / total) + part_in[h, :, cols].astype(jnp.float32) * (keep_l / total)
-            finish(h, b, merged, mem_keys)
-
-    def put_stat(h, b, highest, summed):
-        per = BLOCK // LANES
-        half = stat_buf.shape[1] // 2
-        for e in range(per):
-            cols = slice(e * LANES, (e + 1) * LANES)
-            stat_buf[h, b * per + e : b * per + e + 1, :] = highest[:, cols]
-            stat_buf[h, half + b * per + e : half + b * per + e + 1, :] = summed[:, cols]
+        high_u, sum_u = get_stat(stat_buf, h)
+        high_l, sum_l = get_stat(stat_in, h)
+        highest = jnp.maximum(high_u, high_l)
+        keep_u, keep_l = jnp.exp(high_u - highest), sum_l * jnp.exp(high_l - highest)
+        total = sum_u * keep_u + keep_l
+        merged = acc_buf[h] * (keep_u / total) + part_in[h].astype(jnp.float32) * (keep_l / total)
+        finish(h, merged, cross_buf[h])
 
     def wait_input(h, kind):
         drain(part_bytes, in_sems.at[h, kind])
@@ -243,40 +243,48 @@
         for side in range(2):
             mvt_buf[2 * couple + side] = jnp.concatenate([values_t[side * HS : (side + 1) * HS], ones], axis=0)
 
-    @pl.loop(0, heads)
-    def _(h):
+    def take_keys(h):
         wait_input(h, K)
         wait_input(h, V)
         for j in range(0, span, LANES):
-            kt_buf[j : j + LANES, :] = k_buf[h, :, j : j + LANES].T
-
-        @pl.when(upper == 0)
-        def _():
-            wait_input(h, QU)
-            opposite = {"seq": place + pair}
-            for b in range(blocks):
-                cols = slice(b * BLOCK, (b + 1) * BLOCK)
-                both, summed, highest = attend(kt_buf[...], u_buf[h, :, cols], v_buf[h], False)
-                part_buf[h, :, cols] = (both / summed).astype(jnp.bfloat16)
-                put_stat(h, b, highest, summed)
-                span_cols = pl.ds(b * BLOCK, BLOCK)
-                remote(part_buf.at[h, :, span_cols], part_in.at[h, :, span_cols], part_send, part_sems.at[h], opposite)
-            remote(stat_buf.at[h], stat_in.at[h], stat_send, stat_sems.at[h], opposite)
+            kt_buf[h, j : j + LANES, :] = k_buf[h, :, j : j + LANES].T
+
+    @pl.when(upper == 0)
+    def _():
+        opposite = {"seq": place + pair}
+
+        @pl.loop(0, heads + 1)
+        def _(step):
+            @pl.when(step < heads)
+            def _():
+                h = step
+                take_keys(h)
+                wait_input(h, QU)
+                both, summed, highest = attend(kt_buf[h], u_buf[h], v_buf[h], False)
+                part_buf[h] = (both / summed).astype(jnp.bfloat16)
+                put_stat(h, highest, summed)
+                remote(part_buf.at[h], part_in.at[h], part_send, part_sems.at[h], opposite)
+                remote(stat_buf.at[h], stat_in.at[h], stat_send, stat_sems.at[h], opposite)
+
+            @pl.when(step > 0)
+            def _():
+                h = step - 1
+                wait_input(h, Q)
+                wait_input(h, C)
+                both, summed, _ = causal(h)
+                finish(h, both / summed, cross(h))
+
+    @pl.when(upper == 1)
+    def _():
+        @pl.loop(0, heads)
+        def _(h):
+            take_keys(h)
             wait_input(h, Q)
             wait_input(h, C)
-            mem_keys = memory_keys(h)
-            for b in range(blocks):
-                both, summed, _ = causal_block(h, b)
-                finish(h, b, both / summed, mem_keys)
-
-        @pl.when(upper == 1)
-        def _():
-            wait_input(h, Q)
-            wait_input(h, C)
-            for b in range(blocks):
-                both, summed, highest = causal_block(h, b)
-                acc_buf[h, :, b * BLOCK : (b + 1) * BLOCK] = both
-                put_stat(h, b, highest, summed)
+            both, summed, highest = causal(h)
+            acc_buf[h] = both
+            put_stat(h, highest, summed)
+            cross_buf[h] = cross(h)
 
             @pl.when(h > 0)
             def _():
@@ -328,13 +336,14 @@
         functools.partial(kernel, n_seg, n_seq, n_dp),
         out_shape=jax.ShapeDtypeStruct((features, tokens), bf16),
         in_specs=[pl.BlockSpec(memory_space=pltpu.SMEM)] * 2 + [pl.BlockSpec(memory_space=pl.ANY)] * 6,
-        out_specs=pl.BlockSpec(memory_space=pl.ANY),
+        out_specs=pl.BlockSpec(memory_space=pltpu.VMEM),
         scratch_shapes=[
             wide, wide, pltpu.VMEM((heads, HS + 16, span), bf16), wide, wide,
             relay, relay, memories, memories,
-            pltpu.VMEM((span, 2 * HS), bf16),
+            pltpu.VMEM((heads, span, 2 * HS), bf16),
             pltpu.VMEM((heads, HS + 16, mem_len), bf16),
             block, block, stats, block, stats,
+            pltpu.VMEM((heads, HS, span), f32),
             pltpu.VMEM((heads, HS, span), f32),
             pltpu.VMEM((8, LANES), i32),
             pltpu.VMEM((n_dp, 8, LANES), i32),

time: 72 us -> 65.2 us (0.906)
  the two profiles are of different devices: /device:TPU:184 before, /device:TPU:56 now
where the time goes in v2:
time: 65.2 us; the launch traced here: 65 us
  Pallas kernels  63.1 us (97%)
  local copies, waits for them, and re-layouts  1.87 us (3%)
    pallas_call x1, Pallas kernels, local(): pl.pallas_call(functools.partial(kernel, n_seg, n_seq, n_dp), out_shape=j...  63.1 us
    unnamed x1, local copies, waits for them, and re-layouts  1.87 us

profile of v2, /device:TPU:56, one launch (start us, length us, event | category | flops | bytes accessed | tf_op | source)
XLA Modules:
  0.0 65.0 jit_solution(7952981712695400309)
XLA Ops:
  0.0 63.1 %shard_map.82 = bf16[2048,128]{1,0:T(8,128)(2,1)} custom-call(s32[1,1,2]{2,1,0:T(1,128)} %target_ref.1, s32[1,1,2]{2,1,0:T(1,128)} %source_ref.1, bf16[2048,128]{1,0:T(8,128)(2,1)} %bitcast.12, bf16[2048,128]{1,0:T(8,128)(2,1)} %bitcast.13, bf16[2048,128]{1,0:T(8,128)(2,1)} %bitcast.14, bf16[2048,128]{1,0:T(8,128)(2,1)} %bitcast.15, ...), custom_call_target="tpu_custom_call" | custom-call | tf_op jit(solution)/shard_map/pallas_call | solution.py:335
  63.1 1.9 %copy.10 = bf16[1,1,2048,128]{3,2,1,0:T(8,128)(2,1)} copy(bf16[1,1,2048,128]{3,2,1,0:T(8,128)(2,1)} %bitcast.11) | data formatting | bytes 1048576

commit v3 on v2

--- a/solution.py
+++ b/solution.py
@@ -21,9 +21,9 @@
     target_ref, source_ref, dq_ref, dk_ref, dv_ref, cq_ref, mk_ref, mv_ref,
     out_ref,
     q_buf, k_buf, v_buf, c_buf, u_buf, rk_buf, rv_buf, mk_buf, mv_buf, kt_buf, mvt_buf,
-    o_buf, part_buf, stat_buf, part_in, stat_in, acc_buf, cross_buf, len_own, len_dp, len_ring,
+    o_buf, part_buf, stat_buf, part_in, stat_in, acc_buf, weight_buf, len_own, len_dp, len_ring,
     in_sems, send_sems, relay_sems, relay_sends, mem_sems, mem_sends, part_sems, stat_sems,
-    part_send, stat_send, dp_sem, dp_send, ring_sems, ring_sends, out_sem, out_send,
+    part_send, stat_send, dp_sems, dp_send, ready_sem, ring_sems, ring_sends, out_sem, out_send,
 ):
     group = n_seq // SEQS
     pair = group // 2
@@ -56,9 +56,25 @@
             barrier, 1, device_id={"seq": first + (rank + step) % group}, device_id_type=MESH
         )
 
-    for step in range(1, n_dp):
-        pl.semaphore_signal(barrier, 1, device_id={"dp": (dp + step) % n_dp}, device_id_type=MESH)
-    pl.semaphore_signal(barrier, 1, device_id=early, device_id_type=MESH)
+    order = (dp % 2) * (n_dp // 2) + dp // 2
+
+    def dp_at(turn):
+        return {"dp": (turn % 2) * (n_dp // 2) + turn // 2}
+
+    for turn in range(1, n_dp):
+
+        @pl.when(turn > order)
+        def _():
+            pl.semaphore_signal(barrier, 1, device_id=dp_at(turn), device_id_type=MESH)
+
+    @pl.when(seg < n_seg - 1)
+    def _():
+        pl.semaphore_signal(barrier, 1, device_id=later, device_id_type=MESH)
+
+    @pl.when(seg == 0)
+    def _():
+        pl.semaphore_signal(barrier, 1, device_id=early, device_id_type=MESH)
+
 
     row = lax.broadcasted_iota(jnp.int32, (HS, span), 0)
     column = upper * span + lax.broadcasted_iota(jnp.int32, (HS, span), 1)
@@ -72,9 +88,14 @@
         c_buf[h, (1 - h % 2) * HS : (2 - h % 2) * HS, :] = one_row
     lens = jnp.full(len_own.shape, target_ref[0, 0, 0] + target_ref[0, 0, 1], jnp.int32)
     len_own[...] = lens
-    len_dp[dp] = lens
-
-    pl.semaphore_wait(barrier, group - 1 + n_dp - 1 + 1)
+    len_dp[order] = lens
+
+    first_here = jnp.where(seg > 0, 1, 0) + jnp.where(seg == n_seg - 1, 1, 0)
+    pl.semaphore_wait(barrier, group - 1 + order + first_here)
+
+    @pl.when(seg > 0)
+    def _():
+        pl.semaphore_signal(ready_sem, 1, device_id=early, device_id_type=MESH)
 
     def remote(src, dst, send, recv, device):
         pltpu.make_async_remote_copy(
@@ -87,10 +108,17 @@
     def aligned(start, size):
         return pl.ds(pl.multiple_of(start, size), size)
 
-    for step in range(1, n_dp):
-        remote(len_own, len_dp.at[dp], dp_send, dp_sem, {"dp": (dp + step) % n_dp})
-    for pos, (src, dst) in enumerate(((mk_ref, rk_buf), (mv_ref, rv_buf))):
-        remote(src, dst, relay_sends.at[pos], relay_sems.at[pos], later)
+    def send_lengths(turn):
+        remote(len_own, len_dp.at[order], dp_send, dp_sems.at[order], dp_at(turn))
+
+    def take_lengths(turn):
+        drain(len_dp.at[turn], dp_sems.at[turn])
+
+    for turn in range(n_dp - 1):
+
+        @pl.when(turn < order)
+        def _():
+            send_lengths(turn)
 
     lanes_own = aligned(part * tokens, tokens)
     kinds = {K: (dk_ref, k_buf), V: (dv_ref, v_buf), QU: (dq_ref, u_buf), Q: (dq_ref, q_buf), C: (cq_ref, c_buf)}
@@ -125,11 +153,38 @@
 
     first_kinds, last_kinds = (K, V, QU), (Q, C)
     send_head(0, first_kinds)
-    drain(len_dp.at[pl.ds(1, n_dp - 1)], dp_sem)
+    send_head(1, first_kinds)
+    send_head(0, last_kinds)
+
+    @pl.when(seg < n_seg - 1)
+    def _():
+        pl.semaphore_wait(ready_sem, 1)
+
+    for pos, (src, dst) in enumerate(((mk_ref, rk_buf), (mv_ref, rv_buf))):
+        remote(src, dst, relay_sends.at[pos], relay_sems.at[pos], later)
+    send_head(2, first_kinds)
+    send_head(1, last_kinds)
+    for turn in range(1, n_dp):
+
+        @pl.when(turn > order)
+        def _():
+            take_lengths(turn)
+            send_lengths(turn)
+
+    for turn in range(n_dp - 1):
+
+        @pl.when(turn < order)
+        def _():
+            take_lengths(turn)
+
     len_ring[0] = jnp.sum(len_dp[...], axis=0)
     remote(len_ring.at[0], len_ring.at[1], ring_sends.at[0], ring_sems.at[0], later)
-    send_head(1, first_kinds)
-    send_head(0, last_kinds)
+
+    def pass_lengths(hop):
+        drain(len_ring.at[hop], ring_sems.at[hop - 1])
+        if hop < n_seg - 1:
+            remote(len_ring.at[hop], len_ring.at[hop + 1], ring_sends.at[hop], ring_sems.at[hop], later)
+
     drain(rk_buf, relay_sems.at[0])
     drain(rv_buf, relay_sems.at[1])
     mem_rows = aligned(rank * mem_tokens, mem_tokens)
@@ -150,20 +205,11 @@
             lambda src, dst, pos: remote(src, dst, mem_sends.at[pos], mem_sems.at[pos], {"seq": first + to}),
         )
 
-    for hop in range(1, n_seg):
-        drain(len_ring.at[hop], ring_sems.at[hop - 1])
-        if hop < n_seg - 1:
-            remote(len_ring.at[hop], len_ring.at[hop + 1], ring_sends.at[hop], ring_sems.at[hop], later)
-        if hop == 1:
-            for h in range(2, heads):
-                send_head(h, first_kinds)
-                send_head(h - 1, last_kinds)
-            send_head(heads - 1, last_kinds)
-
-    live = jnp.sum(len_ring[...], axis=0)[0:1]
-    scale = jnp.float32(n_seg * n_dp * SEQS * seq_len) / live.astype(jnp.float32)
-    position = upper * span + lax.broadcasted_iota(jnp.int32, (1, span), 1)
-    weight = jnp.where(position < target, jnp.concatenate([scale] * per, axis=1), 0.0)
+    for h in range(3, heads):
+        send_head(h, first_kinds)
+        send_head(h - 1, last_kinds)
+    send_head(heads - 1, last_kinds)
+    pass_lengths(1)
 
     def attend(keys, queries, values, causal):
         scores = jnp.dot(keys, queries, preferred_element_type=jnp.float32)
@@ -188,7 +234,7 @@
     part_bytes = part_buf.at[0]
 
     def finish(h, self_part, cross_part):
-        o_buf[h] = ((self_part + cross_part) * weight).astype(jnp.bfloat16)
+        o_buf[h] = ((self_part + cross_part) * weight_buf[...]).astype(jnp.bfloat16)
         dst = out_ref.at[pl.ds(pl.multiple_of(part * owned + h * HS, HS), HS)]
         pltpu.make_async_copy(o_buf.at[h, :, lanes_own], dst, out_sem).start()
 
@@ -222,6 +268,8 @@
         return wide
 
     def merge_head(h):
+        wait_input(h, C)
+        cross_part = cross(h)
         drain(part_bytes, part_sems.at[h])
         drain(stat_buf.at[0], stat_sems.at[h])
         high_u, sum_u = get_stat(stat_buf, h)
@@ -230,18 +278,25 @@
         keep_u, keep_l = jnp.exp(high_u - highest), sum_l * jnp.exp(high_l - highest)
         total = sum_u * keep_u + keep_l
         merged = acc_buf[h] * (keep_u / total) + part_in[h].astype(jnp.float32) * (keep_l / total)
-        finish(h, merged, cross_buf[h])
+        finish(h, merged, cross_part)
 
     def wait_input(h, kind):
         drain(part_bytes, in_sems.at[h, kind])
 
-    drain(mk_buf, mem_sems.at[0])
-    drain(mv_buf, mem_sems.at[1])
-    ones = jnp.where(lax.broadcasted_iota(jnp.int32, (16, mem_len), 0) == 0, 1.0, 0.0).astype(jnp.bfloat16)
-    for couple in range(heads // 2):
-        values_t = mv_buf[couple].T
-        for side in range(2):
-            mvt_buf[2 * couple + side] = jnp.concatenate([values_t[side * HS : (side + 1) * HS], ones], axis=0)
+    def take_memory():
+        for hop in range(2, n_seg):
+            pass_lengths(hop)
+        live = jnp.sum(len_ring[...], axis=0)[0:1]
+        scale = jnp.float32(n_seg * n_dp * SEQS * seq_len) / live.astype(jnp.float32)
+        position = upper * span + lax.broadcasted_iota(jnp.int32, (1, span), 1)
+        weight_buf[...] = jnp.where(position < target, jnp.concatenate([scale] * per, axis=1), 0.0)
+        drain(mk_buf, mem_sems.at[0])
+        drain(mv_buf, mem_sems.at[1])
+        ones = jnp.where(lax.broadcasted_iota(jnp.int32, (16, mem_len), 0) == 0, 1.0, 0.0).astype(jnp.bfloat16)
+        for couple in range(heads // 2):
+            values_t = mv_buf[couple].T
+            for side in range(2):
+                mvt_buf[2 * couple + side] = jnp.concatenate([values_t[side * HS : (side + 1) * HS], ones], axis=0)
 
     def take_keys(h):
         wait_input(h, K)
@@ -266,6 +321,10 @@
                 remote(part_buf.at[h], part_in.at[h], part_send, part_sems.at[h], opposite)
                 remote(stat_buf.at[h], stat_in.at[h], stat_send, stat_sems.at[h], opposite)
 
+            @pl.when(step == 1)
+            def _():
+                take_memory()
+
             @pl.when(step > 0)
             def _():
                 h = step - 1
@@ -280,11 +339,13 @@
         def _(h):
             take_keys(h)
             wait_input(h, Q)
-            wait_input(h, C)
             both, summed, highest = causal(h)
             acc_buf[h] = both
             put_stat(h, highest, summed)
-            cross_buf[h] = cross(h)
+
+            @pl.when(h == 1)
+            def _():
+                take_memory()
 
             @pl.when(h > 0)
             def _():
@@ -344,12 +405,12 @@
             pltpu.VMEM((heads, HS + 16, mem_len), bf16),
             block, block, stats, block, stats,
             pltpu.VMEM((heads, HS, span), f32),
-            pltpu.VMEM((heads, HS, span), f32),
+            pltpu.VMEM((1, span), f32),
             pltpu.VMEM((8, LANES), i32),
             pltpu.VMEM((n_dp, 8, LANES), i32),
             pltpu.VMEM((n_seg, 8, LANES), i32),
             dma((heads, 5)), dma((5,)), dma((2,)), dma((2,)), dma((2,)), dma((2,)), dma((heads,)), dma((heads,)),
-            dma, dma, dma, dma, dma((n_seg,)), dma((n_seg,)), dma, dma,
+            dma, dma, dma((n_dp,)), dma, pltpu.SemaphoreType.REGULAR, dma((n_seg,)), dma((n_seg,)), dma, dma,
         ],
         compiler_params=pltpu.CompilerParams(
             collective_id=0, has_side_effects=True, vmem_limit_bytes=56 * 2**20

time: 65.2 us -> 62.1 us (0.952)
  Pallas kernels: 63.1 us -> 60.1 us
    pallas_call x1, Pallas kernels: 63.1 us -> 60.1 us  [local(): pl.pallas_call(functools.partial(kernel, n_seg, n_seq, n_dp), out_shape=j...]
where the time goes in v3:
time: 62.1 us; the launch traced here: 62 us
  Pallas kernels  60.1 us (97%)
  local copies, waits for them, and re-layouts  1.87 us (3%)
    pallas_call x1, Pallas kernels, local(): pl.pallas_call(functools.partial(kernel, n_seg, n_seq, n_dp), out_shape=j...  60.1 us
    unnamed x1, local copies, waits for them, and re-layouts  1.87 us

profile of v3, /device:TPU:56, one launch (start us, length us, event | category | flops | bytes accessed | tf_op | source)
XLA Modules:
  0.0 62.0 jit_solution(8242462398977960397)
XLA Ops:
  0.0 60.1 %shard_map.82 = bf16[2048,128]{1,0:T(8,128)(2,1)} custom-call(s32[1,1,2]{2,1,0:T(1,128)} %target_ref.1, s32[1,1,2]{2,1,0:T(1,128)} %source_ref.1, bf16[2048,128]{1,0:T(8,128)(2,1)} %bitcast.12, bf16[2048,128]{1,0:T(8,128)(2,1)} %bitcast.13, bf16[2048,128]{1,0:T(8,128)(2,1)} %bitcast.14, bf16[2048,128]{1,0:T(8,128)(2,1)} %bitcast.15, ...), custom_call_target="tpu_custom_call" | custom-call | tf_op jit(solution)/shard_map/pallas_call | solution.py:396
  60.1 1.9 %copy.10 = bf16[1,1,2048,128]{3,2,1,0:T(8,128)(2,1)} copy(bf16[1,1,2048,128]{3,2,1,0:T(8,128)(2,1)} %bitcast.11) | data formatting | bytes 1048576

commit v4 on v3

--- a/solution.py
+++ b/solution.py
@@ -18,12 +18,12 @@
 
 def kernel(
     n_seg, n_seq, n_dp,
-    target_ref, source_ref, dq_ref, dk_ref, dv_ref, cq_ref, mk_ref, mv_ref,
+    target_hbm, source_hbm, dq_ref, dk_ref, dv_ref, cq_ref, mk_ref, mv_ref,
     out_ref,
     q_buf, k_buf, v_buf, c_buf, u_buf, rk_buf, rv_buf, mk_buf, mv_buf, kt_buf, mvt_buf,
     o_buf, part_buf, stat_buf, part_in, stat_in, acc_buf, weight_buf, len_own, len_dp, len_ring,
     in_sems, send_sems, relay_sems, relay_sends, mem_sems, mem_sends, part_sems, stat_sems,
-    part_send, stat_send, dp_sems, dp_send, ready_sem, ring_sems, ring_sends, out_sem, out_send,
+    part_send, stat_send, dp_sems, dp_send, ready_sem, lower_sem, target_ref, source_ref, smem_sems, ring_sems, ring_sends, out_sem, out_send,
 ):
     group = n_seq // SEQS
     pair = group // 2
@@ -34,7 +34,7 @@
     heads = q_buf.shape[0]
     owned = heads * HS
     blocks = span // BLOCK
-    per = span // LANES
+    per = BLOCK // LANES
 
     seg, place, dp = lax.axis_index("segment"), lax.axis_index("seq"), lax.axis_index("dp")
     which = place // group
@@ -43,18 +43,22 @@
     upper = rank // pair
     part = rank % pair
     base = first + upper * pair
-    target = target_ref[0, 0, which]
-    source = source_ref[0, 0, which]
     later = {"segment": (seg + 1) % n_seg}
     early = {"segment": (seg + n_seg - 1) % n_seg}
 
     barrier = pltpu.get_barrier_semaphore()
 
-    @pl.loop(1, group)
+    @pl.loop(1, pair)
     def _(step):
         pl.semaphore_signal(
-            barrier, 1, device_id={"seq": first + (rank + step) % group}, device_id_type=MESH
+            barrier, 1, device_id={"seq": base + (part + step) % pair}, device_id_type=MESH
         )
+
+    @pl.when(upper == 1)
+    def _():
+        @pl.loop(0, pair)
+        def _(step):
+            pl.semaphore_signal(barrier, 1, device_id={"seq": first + step}, device_id_type=MESH)
 
     order = (dp % 2) * (n_dp // 2) + dp // 2
 
@@ -75,6 +79,17 @@
     def _():
         pl.semaphore_signal(barrier, 1, device_id=early, device_id_type=MESH)
 
+
+    lengths = [
+        pltpu.make_async_copy(src, dst, smem_sems.at[pos])
+        for pos, (src, dst) in enumerate(((target_hbm, target_ref), (source_hbm, source_ref)))
+    ]
+    for copy in lengths:
+        copy.start()
+    for copy in lengths:
+        copy.wait()
+    target = target_ref[0, 0, which]
+    source = source_ref[0, 0, which]
 
     row = lax.broadcasted_iota(jnp.int32, (HS, span), 0)
     column = upper * span + lax.broadcasted_iota(jnp.int32, (HS, span), 1)
@@ -91,7 +106,14 @@
     len_dp[order] = lens
 
     first_here = jnp.where(seg > 0, 1, 0) + jnp.where(seg == n_seg - 1, 1, 0)
-    pl.semaphore_wait(barrier, group - 1 + order + first_here)
+    upper_here = pair * (1 - upper)
+    pl.semaphore_wait(barrier, pair - 1 + upper_here + order + first_here)
+
+    @pl.when(upper == 0)
+    def _():
+        @pl.loop(0, pair)
+        def _(step):
+            pl.semaphore_signal(lower_sem, 1, device_id={"seq": first + pair + step}, device_id_type=MESH)
 
     @pl.when(seg > 0)
     def _():
@@ -152,7 +174,13 @@
                 remote(rows(to), dst, send_sems.at[kind], sem, {"seq": base + to})
 
     first_kinds, last_kinds = (K, V, QU), (Q, C)
-    send_head(0, first_kinds)
+    send_head(0, (K, V))
+
+    @pl.when(upper == 1)
+    def _():
+        pl.semaphore_wait(lower_sem, pair)
+
+    send_head(0, (QU,))
     send_head(1, first_kinds)
     send_head(0, last_kinds)
 
@@ -233,23 +261,27 @@
     token = lax.broadcasted_iota(jnp.int32, (mem_len, LANES), 0)
     part_bytes = part_buf.at[0]
 
-    def finish(h, self_part, cross_part):
-        o_buf[h] = ((self_part + cross_part) * weight_buf[...]).astype(jnp.bfloat16)
+    def columns(b):
+        return slice(b * BLOCK, (b + 1) * BLOCK)
+
+    def finish(h, b, self_part, cross_part):
+        mixed = (self_part + cross_part[:, columns(b)]) * weight_buf[:, columns(b)]
+        o_buf[h, :, columns(b)] = mixed.astype(jnp.bfloat16)
         dst = out_ref.at[pl.ds(pl.multiple_of(part * owned + h * HS, HS), HS)]
-        pltpu.make_async_copy(o_buf.at[h, :, lanes_own], dst, out_sem).start()
-
-        @pl.loop(1, pair)
-        def _(step):
-            to = (part + step) % pair
-            remote(o_buf.at[h, :, aligned(to * tokens, tokens)], dst, out_send, out_sem, {"seq": base + to})
+        for to in range(b * per, (b + 1) * per):
+            src = o_buf.at[h, :, pl.ds(to * tokens, tokens)]
+
+            @pl.when(part != to)
+            def _():
+                remote(src, dst, out_send, out_sem, {"seq": base + to})
+
+            @pl.when(part == to)
+            def _():
+                pltpu.make_async_copy(src, dst, out_sem).start()
 
     def cross(h):
         both, summed, _ = attend(memory_keys(h), c_buf[h], mvt_buf[h], False)
         return both / summed
-
-    def causal(h):
-        pieces = [causal_block(h, b) for b in range(blocks)]
-        return [jnp.concatenate([piece[k] for piece in pieces], axis=1) for k in range(3)]
 
     def memory_keys(h):
         side = h % 2
@@ -257,28 +289,32 @@
         mask = jnp.where((lane == (1 - side) * HS) & (token >= source), MASKED, 0.0)
         return jnp.where(inside, mk_buf[h // 2], mask.astype(jnp.bfloat16))
 
-    def put_stat(h, highest, summed):
+    def put_stat(h, b, highest, summed):
         for e in range(per):
             cols = slice(e * LANES, (e + 1) * LANES)
-            stat_buf[h, e : e + 1, :] = highest[:, cols]
-            stat_buf[h, per + e : per + e + 1, :] = summed[:, cols]
-
-    def get_stat(ref, h):
-        wide = [jnp.concatenate([ref[h, at + e : at + e + 1, :] for e in range(per)], axis=1) for at in (0, per)]
-        return wide
+            stat_buf[h * blocks + b, e : e + 1, :] = highest[:, cols]
+            stat_buf[h * blocks + b, per + e : per + e + 1, :] = summed[:, cols]
+
+    def get_stat(ref, h, b):
+        return [
+            jnp.concatenate([ref[h * blocks + b, at + e : at + e + 1, :] for e in range(per)], axis=1)
+            for at in (0, per)
+        ]
 
     def merge_head(h):
         wait_input(h, C)
         cross_part = cross(h)
-        drain(part_bytes, part_sems.at[h])
-        drain(stat_buf.at[0], stat_sems.at[h])
-        high_u, sum_u = get_stat(stat_buf, h)
-        high_l, sum_l = get_stat(stat_in, h)
-        highest = jnp.maximum(high_u, high_l)
-        keep_u, keep_l = jnp.exp(high_u - highest), sum_l * jnp.exp(high_l - highest)
-        total = sum_u * keep_u + keep_l
-        merged = acc_buf[h] * (keep_u / total) + part_in[h].astype(jnp.float32) * (keep_l / total)
-        finish(h, merged, cross_part)
+        for b in range(blocks):
+            drain(part_bytes.at[:, pl.ds(0, BLOCK)], part_sems.at[h * blocks + b])
+            drain(stat_buf.at[0], stat_sems.at[h * blocks + b])
+            high_u, sum_u = get_stat(stat_buf, h, b)
+            high_l, sum_l = get_stat(stat_in, h, b)
+            highest = jnp.maximum(high_u, high_l)
+            keep_u, keep_l = jnp.exp(high_u - highest), sum_l * jnp.exp(high_l - highest)
+            total = sum_u * keep_u + keep_l
+            other = part_in[h, :, columns(b)].astype(jnp.float32)
+            merged = acc_buf[h, :, columns(b)] * (keep_u / total) + other * (keep_l / total)
+            finish(h, b, merged, cross_part)
 
     def wait_input(h, kind):
         drain(part_bytes, in_sems.at[h, kind])
@@ -289,7 +325,7 @@
         live = jnp.sum(len_ring[...], axis=0)[0:1]
         scale = jnp.float32(n_seg * n_dp * SEQS * seq_len) / live.astype(jnp.float32)
         position = upper * span + lax.broadcasted_iota(jnp.int32, (1, span), 1)
-        weight_buf[...] = jnp.where(position < target, jnp.concatenate([scale] * per, axis=1), 0.0)
+        weight_buf[...] = jnp.where(position < target, jnp.concatenate([scale] * (span // LANES), axis=1), 0.0)
         drain(mk_buf, mem_sems.at[0])
         drain(mv_buf, mem_sems.at[1])
         ones = jnp.where(lax.broadcasted_iota(jnp.int32, (16, mem_len), 0) == 0, 1.0, 0.0).astype(jnp.bfloat16)
@@ -315,11 +351,16 @@
                 h = step
                 take_keys(h)
                 wait_input(h, QU)
-                both, summed, highest = attend(kt_buf[h], u_buf[h], v_buf[h], False)
-                part_buf[h] = (both / summed).astype(jnp.bfloat16)
-                put_stat(h, highest, summed)
-                remote(part_buf.at[h], part_in.at[h], part_send, part_sems.at[h], opposite)
-                remote(stat_buf.at[h], stat_in.at[h], stat_send, stat_sems.at[h], opposite)
+                for b in range(blocks):
+                    both, summed, highest = attend(kt_buf[h], u_buf[h, :, columns(b)], v_buf[h], False)
+                    part_buf[h, :, columns(b)] = (both / summed).astype(jnp.bfloat16)
+                    put_stat(h, b, highest, summed)
+                    index = h * blocks + b
+                    cols = pl.ds(b * BLOCK, BLOCK)
+                    remote(
+                        part_buf.at[h, :, cols], part_in.at[h, :, cols], part_send, part_sems.at[index], opposite
+                    )
+                    remote(stat_buf.at[index], stat_in.at[index], stat_send, stat_sems.at[index], opposite)
 
             @pl.when(step == 1)
             def _():
@@ -330,8 +371,10 @@
                 h = step - 1
                 wait_input(h, Q)
                 wait_input(h, C)
-                both, summed, _ = causal(h)
-                finish(h, both / summed, cross(h))
+                cross_part = cross(h)
+                for b in range(blocks):
+                    both, summed, _ = causal_block(h, b)
+                    finish(h, b, both / summed, cross_part)
 
     @pl.when(upper == 1)
     def _():
@@ -339,9 +382,10 @@
         def _(h):
             take_keys(h)
             wait_input(h, Q)
-            both, summed, highest = causal(h)
-            acc_buf[h] = both
-            put_stat(h, highest, summed)
+            for b in range(blocks):
+                both, summed, highest = causal_block(h, b)
+                acc_buf[h, :, columns(b)] = both
+                put_stat(h, b, highest, summed)
 
             @pl.when(h == 1)
             def _():
@@ -390,14 +434,15 @@
     dma = pltpu.SemaphoreType.DMA
     wide = pltpu.VMEM((heads, 2 * HS, span), bf16)
     block = pltpu.VMEM((heads, HS, span), bf16)
-    stats = pltpu.VMEM((heads, 2 * span // LANES, LANES), f32)
+    blocks = span // BLOCK
+    stats = pltpu.VMEM((heads * blocks, 2 * BLOCK // LANES, LANES), f32)
     relay = pltpu.VMEM((mem_tokens, features), bf16)
     memories = pltpu.VMEM((heads // 2, mem_len, LANES), bf16)
     out = pl.pallas_call(
         functools.partial(kernel, n_seg, n_seq, n_dp),
         out_shape=jax.ShapeDtypeStruct((features, tokens), bf16),
-        in_specs=[pl.BlockSpec(memory_space=pltpu.SMEM)] * 2 + [pl.BlockSpec(memory_space=pl.ANY)] * 6,
-        out_specs=pl.BlockSpec(memory_space=pltpu.VMEM),
+        in_specs=[pl.BlockSpec(memory_space=pl.ANY)] * 8,
+        out_specs=pl.BlockSpec(memory_space=pl.ANY),
         scratch_shapes=[
             wide, wide, pltpu.VMEM((heads, HS + 16, span), bf16), wide, wide,
             relay, relay, memories, memories,
@@ -409,8 +454,10 @@
             pltpu.VMEM((8, LANES), i32),
             pltpu.VMEM((n_dp, 8, LANES), i32),
             pltpu.VMEM((n_seg, 8, LANES), i32),
-            dma((heads, 5)), dma((5,)), dma((2,)), dma((2,)), dma((2,)), dma((2,)), dma((heads,)), dma((heads,)),
-            dma, dma, dma((n_dp,)), dma, pltpu.SemaphoreType.REGULAR, dma((n_seg,)), dma((n_seg,)), dma, dma,
+            dma((heads, 5)), dma((5,)), dma((2,)), dma((2,)), dma((2,)), dma((2,)), dma((heads * blocks,)), dma((heads * blocks,)),
+            dma, dma, dma((n_dp,)), dma, pltpu.SemaphoreType.REGULAR, pltpu.SemaphoreType.REGULAR,
+            pltpu.SMEM((1, 1, SEQS), i32), pltpu.SMEM((1, 1, SEQS), i32), dma((2,)),
+            dma((n_seg,)), dma((n_seg,)), dma, dma,
         ],
         compiler_params=pltpu.CompilerParams(
             collective_id=0, has_side_effects=True, vmem_limit_bytes=56 * 2**20

time: 62.1 us -> 59.7 us (0.961)
  Pallas kernels: 60.1 us -> 57.7 us
    pallas_call x1, Pallas kernels: 60.1 us -> 57.7 us  [local(): pl.pallas_call(functools.partial(kernel, n_seg, n_seq, n_dp), out_shape=j...]
where the time goes in v4:
time: 59.7 us; the launch traced here: 59.6 us
  Pallas kernels  57.7 us (97%)
  local copies, waits for them, and re-layouts  1.87 us (3%)
    pallas_call x1, Pallas kernels, local(): pl.pallas_call(functools.partial(kernel, n_seg, n_seq, n_dp), out_shape=j...  57.7 us
    unnamed x1, local copies, waits for them, and re-layouts  1.87 us

profile of v4, /device:TPU:56, one launch (start us, length us, event | category | flops | bytes accessed | tf_op | source)
XLA Modules:
  0.0 59.6 jit_solution(16544885616002955820)
XLA Ops:
  0.0 57.7 %shard_map.82 = bf16[2048,128]{1,0:T(8,128)(2,1)} custom-call(s32[1,1,2]{2,1,0:T(1,128)} %target_hbm.1, s32[1,1,2]{2,1,0:T(1,128)} %source_hbm.1, bf16[2048,128]{1,0:T(8,128)(2,1)} %bitcast.12, bf16[2048,128]{1,0:T(8,128)(2,1)} %bitcast.13, bf16[2048,128]{1,0:T(8,128)(2,1)} %bitcast.14, bf16[2048,128]{1,0:T(8,128)(2,1)} %bitcast.15, ...), custom_call_target="tpu_custom_call" | custom-call | tf_op jit(solution)/shard_map/pallas_call | solution.py:441
  57.7 1.9 %copy.10 = bf16[1,1,2048,128]{3,2,1,0:T(8,128)(2,1)} copy(bf16[1,1,2048,128]{3,2,1,0:T(8,128)(2,1)} %bitcast.11) | data formatting | bytes 1048576

commit v5 on v4

--- a/solution.py
+++ b/solution.py
@@ -168,9 +168,9 @@
 
             pltpu.make_async_copy(rows(part), dst, sem).start()
 
-            @pl.loop(1, pair)
+            @pl.loop(0, pair - 1)
             def _(step):
-                to = (part + step) % pair
+                to = (part + 1 + (step + pair // 2 - 1) % (pair - 1)) % pair
                 remote(rows(to), dst, send_sems.at[kind], sem, {"seq": base + to})
 
     first_kinds, last_kinds = (K, V, QU), (Q, C)

time: 59.7 us -> 59.7 us (level)
  no operation moved by 1% of the time
where the time goes in v5:
time: 59.7 us; the launch traced here: 59.5 us
  Pallas kernels  57.6 us (96%)
  local copies, waits for them, and re-layouts  1.87 us (3%)
    pallas_call x1, Pallas kernels, local(): pl.pallas_call(functools.partial(kernel, n_seg, n_seq, n_dp), out_shape=j...  57.6 us
    unnamed x1, local copies, waits for them, and re-layouts  1.87 us

profile of v5, /device:TPU:56, one launch (start us, length us, event | category | flops | bytes accessed | tf_op | source)
XLA Modules:
  0.0 59.5 jit_solution(4542147519309880479)
XLA Ops:
  0.0 57.6 %shard_map.82 = bf16[2048,128]{1,0:T(8,128)(2,1)} custom-call(s32[1,1,2]{2,1,0:T(1,128)} %target_hbm.1, s32[1,1,2]{2,1,0:T(1,128)} %source_hbm.1, bf16[2048,128]{1,0:T(8,128)(2,1)} %bitcast.12, bf16[2048,128]{1,0:T(8,128)(2,1)} %bitcast.13, bf16[2048,128]{1,0:T(8,128)(2,1)} %bitcast.14, bf16[2048,128]{1,0:T(8,128)(2,1)} %bitcast.15, ...), custom_call_target="tpu_custom_call" | custom-call | tf_op jit(solution)/shard_map/pallas_call | solution.py:441
  57.6 1.9 %copy.10 = bf16[1,1,2048,128]{3,2,1,0:T(8,128)(2,1)} copy(bf16[1,1,2048,128]{3,2,1,0:T(8,128)(2,1)} %bitcast.11) | data formatting | bytes 1048576

commit v6 on v5

--- a/solution.py
+++ b/solution.py
@@ -173,7 +173,7 @@
                 to = (part + 1 + (step + pair // 2 - 1) % (pair - 1)) % pair
                 remote(rows(to), dst, send_sems.at[kind], sem, {"seq": base + to})
 
-    first_kinds, last_kinds = (K, V, QU), (Q, C)
+    first_kinds, last_kinds = (QU, K, V), (Q, C)
     send_head(0, (K, V))
 
     @pl.when(upper == 1)

time: 59.7 us -> 59.6 us (level)
  no operation moved by 1% of the time
where the time goes in v6:
time: 59.6 us; the launch traced here: 59.4 us
  Pallas kernels  57.5 us (96%)
  local copies, waits for them, and re-layouts  1.87 us (3%)
    pallas_call x1, Pallas kernels, local(): pl.pallas_call(functools.partial(kernel, n_seg, n_seq, n_dp), out_shape=j...  57.5 us
    unnamed x1, local copies, waits for them, and re-layouts  1.87 us

profile of v6, /device:TPU:56, one launch (start us, length us, event | category | flops | bytes accessed | tf_op | source)
XLA Modules:
  0.0 59.4 jit_solution(6963902628440737653)
XLA Ops:
  0.0 57.5 %shard_map.82 = bf16[2048,128]{1,0:T(8,128)(2,1)} custom-call(s32[1,1,2]{2,1,0:T(1,128)} %target_hbm.1, s32[1,1,2]{2,1,0:T(1,128)} %source_hbm.1, bf16[2048,128]{1,0:T(8,128)(2,1)} %bitcast.12, bf16[2048,128]{1,0:T(8,128)(2,1)} %bitcast.13, bf16[2048,128]{1,0:T(8,128)(2,1)} %bitcast.14, bf16[2048,128]{1,0:T(8,128)(2,1)} %bitcast.15, ...), custom_call_target="tpu_custom_call" | custom-call | tf_op jit(solution)/shard_map/pallas_call | solution.py:441
  57.5 1.9 %copy.10 = bf16[1,1,2048,128]{3,2,1,0:T(8,128)(2,1)} copy(bf16[1,1,2048,128]{3,2,1,0:T(8,128)(2,1)} %bitcast.11) | data formatting | bytes 1048576
